TPU v7x, 128 devices: a whole 4x4x4 slice. The times are simulated.
128 devices in a mesh: rows: 8 (over z, x_lo), vocab: 16 (over x_hi, y, core).
Axes of the slice: x: 4 (x_hi: 2, x_lo: 2; x = x_hi * 2 + x_lo), y: 4, z: 4, core: 2. Of those that a mesh axis runs over, the one named last changes fastest.
Arguments:
- hidden: bfloat16 [4096, 4096], P('rows', 'vocab')
- lexicon_projection_weights: bfloat16 [4096, 38912], P(None, 'vocab')
- sampled: int32 [4096], P('rows'), may hold values from 0 to 38911, as said below
- keep_bits: int32 [4096, 16], P('rows', 'vocab'), may hold values from 0 to 524287, as said below
Outputs:
- full_logprob: float32 [4096], P('rows')
- retained_log_chance: float32 [4096], P('rows')
- mean_gap: float32 [], replicated
Inputs may be any that keep to these rules, and one draw needn't show every extreme that they name: sampled[t] is kept: its keep block's bit is set in keep_bits of its row. `keep_bits`: only the lowest 19 bits are used.
All inputs are finite; a program needn't handle non-finite values.
Results may differ from a plain program's by a relative error of at most 0.0003.
Values may be sent and summed in bfloat16 or wider, within the bound.
A program may use at most 128 MiB of HBM per device.

v0:
```python
import jax
import jax.numpy as jnp
from jax import lax
from jax.sharding import PartitionSpec as P

VBLK = 128


softness_divisor = 0.7
absent = -1e30


def per_device(hidden, lexicon_projection_weights, sampled, keep_bits):
    rows_here = hidden.shape[0]
    width = lexicon_projection_weights.shape[1]
    whole = lax.all_gather(hidden, "vocab", axis=1, tiled=True)
    plain_energy_values = jnp.dot(
        whole, lexicon_projection_weights, preferred_element_type=jnp.float32
    )
    raw_preference_values = plain_energy_values / softness_divisor
    offset = lax.axis_index("vocab") * width
    local_ids = sampled - offset
    columns = lax.broadcasted_iota(jnp.int32, (rows_here, width), 1)
    picked = jnp.sum(jnp.where(columns == local_ids[:, None], raw_preference_values, 0.0), axis=1)
    block_number = width // VBLK
    shift_amounts = jnp.arange(block_number, dtype=jnp.int32)
    blocks = jnp.right_shift(keep_bits, shift_amounts[None, :]) & 1
    keep = jnp.broadcast_to(blocks[:, :, None], (rows_here, block_number, VBLK)).reshape(
        rows_here, width
    )
    is_kept = keep == 1
    full_top = jnp.max(raw_preference_values, axis=1)
    kept_top = jnp.max(jnp.where(is_kept, raw_preference_values, absent), axis=1)
    full_max, kept_max = lax.pmax((full_top, kept_top), "vocab")
    full_sum = jnp.sum(jnp.exp(raw_preference_values - full_max[:, None]), axis=1)
    kept_sum = jnp.sum(
        jnp.where(is_kept, jnp.exp(raw_preference_values - kept_max[:, None]), 0.0), axis=1
    )
    full_sum, kept_sum, selected_everything = lax.psum((full_sum, kept_sum, picked), "vocab")
    full_logprob = selected_everything - (full_max + jnp.log(full_sum))
    retained_log_chance = selected_everything - (kept_max + jnp.log(kept_sum))
    gap_total = lax.psum(jnp.sum(retained_log_chance - full_logprob), "rows")
    mean_gap = gap_total / (rows_here * lax.axis_size("rows"))
    return (full_logprob, retained_log_chance, mean_gap)


def solution(mesh):
    placed = (P("rows", "vocab"), P(None, "vocab"), P("rows"), P("rows", "vocab"))
    return jax.shard_map(
        per_device,
        mesh=mesh,
        in_specs=placed,
        out_specs=(P("rows"), P("rows"), P()),
        check_vma=False,
    )
```

profile of v0, /device:TPU:1, one launch (start us, length us, event | category | flops | bytes accessed | tf_op | source)
XLA Modules:
  0.0 187.2 jit_solution(4195992394929841576)
XLA Ops:
  7.2 0.0 all-gather.2.cloned.1.call-start
  7.2 0.7 all-gather.2.cloned.1.call-update
  7.9 0.7 and_compare_fusion
  8.6 0.3 broadcast_in_dim.19
  8.9 1.4 copy.7
  10.3 0.7 broadcast_subtract_fusion
  11.0 59.5 %all-gather.2.cloned.1.call-done = bf16[512,4096]{1,0:T(8,128)(2,1)} async-done(((bf16[512,256]{1,0:T(8,128)(2,1)}), bf16[512,4096]{1,0:T(8,128)(2,1)}) %all-gather.2.cloned.1.call-update) | async-done | bytes 4194320 | tf_op jit(solution)/shard_map/all_gather | solution.py:16
  70.5 18.6 %select_reduce_fusion.1 = (f32[512]{0:T(512)S(1)}, f32[512]{0:T(512)S(1)}, f32[512,2432]{1,0:T(8,128)}) fusion(pred[512,2432]{1,0:T(32,128)(4,1)S(1)} %copy.7, bf16[512,4096]{1,0:T(8,128)(2,1)} %all-gather.2.cloned.1.call-done, bf16[4096,2432]{1,0:T(8,128)(2,1)} %param.5), kind=kOutput, calls=%fused_computation.2 | convolution fusion | flops 10205528064 | bytes 30347264 | tf_op jit(solution)/shard_map/dot_general | solution.py:17
  89.2 32.8 %all-reduce.1 = (f32[512]{0:T(512)S(1)}, f32[512]{0:T(512)S(1)}) all-reduce(f32[512]{0:T(512)S(1)} %get-tuple-element.6, f32[512]{0:T(512)S(1)} %get-tuple-element.7), channel_id=1, replica_groups=mesh['rows'=8,'vocab'=16] {'vocab'}, use_global_device_ids=true, to_apply=%region_7.8 | all-reduce | flops 1024 | bytes 8192 | tf_op jit(solution)/shard_map/pmax | solution.py:34
  121.9 4.4 %select_reduce_fusion = (f32[512]{0:T(512)S(1)}, f32[512]{0:T(512)S(1)}, f32[512]{0:T(512)S(1)}) fusion(pred[512,2432]{1,0:T(32,128)(4,1)S(1)} %copy.7, f32[512,2432]{1,0:T(8,128)} %get-tuple-element.16, f32[512]{0:T(512)S(1)} %get-tuple-element.11, f32[512]{0:T(512)S(1)} %get-tuple-element.12, s32[512]{0:T(512)S(1)} %broadcast_subtract_fusion), kind=kLoop, calls=%fused_computation.1 | loop fusion | flops 9959936 | bytes 6238208 | tf_op jit(solution)/shard_map/reduce_sum | solution.py:36
  126.4 34.3 %all-reduce = (f32[512]{0:T(512)S(1)}, f32[512]{0:T(512)S(1)}, f32[512]{0:T(512)S(1)}) all-reduce(f32[512]{0:T(512)S(1)} %get-tuple-element.5, f32[512]{0:T(512)S(1)} %get-tuple-element.4, f32[512]{0:T(512)S(1)} %get-tuple-element.3), channel_id=1, replica_groups=mesh['rows'=8,'vocab'=16] {'vocab'}, use_global_device_ids=true, to_apply=%region_1.2 | all-reduce | flops 1536 | bytes 12288 | tf_op jit(solution)/shard_map/psum | solution.py:39
  160.6 1.2 subtract_reduce_fusion
  161.8 16.8 %psum.31 = f32[]{:T(128)} all-reduce(f32[]{:T(128)} %get-tuple-element.13), channel_id=1, replica_groups=mesh['rows'=8,'vocab'=16] {'rows'}, use_global_device_ids=true, to_apply=%region_11.12 | all-reduce | flops 1 | bytes 8 | tf_op jit(solution)/shard_map/psum | solution.py:42
Async XLA Ops:
  7.2 63.4 %all-gather.2.cloned.1.call-start = ((), (), s32[]{:S(2)}) async-start(), calls=%async_computation | async-start | bytes 4456448 | tf_op jit(solution)/shard_map/all_gather | solution.py:16
Sparse Core Ops, SparseCore 0:
  10.3 60.2 all-gather.1
where the time goes:
time: 190 us; the launch traced here: 187 us
  blocking collectives  83.8 us (44%)
  waiting for transfers between devices  60.2 us (32%)
  matrix products  18.6 us (10%)
  between operations  15.8 us (8%)
  other arithmetic  7.02 us (4%)
    all_gather x1, waiting for transfers between devices, per_device(): whole = lax.all_gather(hidden, 'vocab', axis=1, tiled=True)  59.5 us
    psum x1, blocking collectives, per_device(): lax.psum((full_sum, kept_sum, picked), 'vocab')  34.3 us
    pmax x1, blocking collectives, per_device(): full_max, kept_max = lax.pmax((full_top, kept_top), 'vocab')  32.8 us
    dot_general x1, matrix products, per_device(): jnp.dot(whole, lexicon_projection_weights, preferred_element_type=jnp.flo...  18.6 us
    psum x1, blocking collectives, per_device(): gap_total = lax.psum(jnp.sum(retained_log_chance - full_logprob), 'rows')  16.8 us
    reduce_sum x1, other arithmetic, per_device(): jnp.sum(jnp.where(is_kept, jnp.exp(raw_preference_values - kept_max[:, No...  4.45 us
  transfers between devices with their start and end apart: 1, of which 1 were waited for; matrix products, arithmetic and copies ran while one was open for 2% of the time, Pallas kernels for 0%

commit v1 on v0

v1 whole, which is shorter than its diff:
```python
import jax
import jax.numpy as jnp
from jax import lax
from jax.experimental import pallas as pl
from jax.experimental.pallas import tpu as pltpu
from jax.sharding import PartitionSpec as P

MESH = pl.DeviceIdType.MESH
F32 = jnp.float32

SOFTNESS = 0.7
LOG2E = 1.4426950408889634
EXP_SCALE = LOG2E / SOFTNESS
ABSENT = -2.3819e38

TOKENS = 4096
ROWS = 512
FEAT = 256
CHIP_FEAT = 512
CHIPS = 8
WIDTH = 2432
VBLK = 128
NBLK = 19
TILE = 256
Q = 128
NQ = 4
N_VOCAB = 16
N_ROWS = 8

OWN, UP, DOWN, FAR = (0, 0), (0, 1), (0, 3), (0, 2)
XOWN, XUP, XDOWN, XFAR = (1, 0), (1, 1), (1, 3), (1, 2)

LINKS = {"+": (0, 1), "-": (0, 3), "x": (1, 0)}


def seen_by(chunk, link):
    dx, dy = LINKS[link]
    return ((chunk[0] + dx) % 2, (chunk[1] - dy) % 4)


PROGRAM = [
    ("send", "+", OWN, 0), ("send", "-", OWN, 0), ("send", "x", OWN, 0),
    ("send", "+", OWN, 1), ("send", "-", OWN, 1), ("send", "x", OWN, 1),
    ("send", "+", OWN, 2), ("send", "-", OWN, 2), ("send", "x", OWN, 2),
    ("send", "x", OWN, 3),
    ("own",),
    ("got", UP, 0), ("got", DOWN, 0), ("got", XOWN, 0),
    ("send", "+", DOWN, 0), ("send", "+", OWN, 3),
    ("got", UP, 1), ("got", DOWN, 1), ("got", XOWN, 1),
    ("send", "-", UP, 1), ("send", "-", OWN, 3),
    ("mul", 0, 128, (UP, DOWN, XOWN)),
    ("got", UP, 2), ("got", DOWN, 2), ("got", XOWN, 2),
    ("send", "+", DOWN, 2), ("send", "+", XOWN, 0), ("send", "+", XOWN, 1),
    ("send", "-", XOWN, 0), ("send", "-", XOWN, 1),
    ("mul", 128, 128, (UP, DOWN, XOWN)),
    ("got", FAR, 0), ("got", FAR, 1), ("got", XOWN, 3),
    ("send", "x", FAR, 0), ("send", "x", FAR, 1),
    ("send", "+", XOWN, 2), ("send", "+", XOWN, 3),
    ("mul", 256, 128, (UP, DOWN, XOWN)),
    ("got", UP, 3), ("got", DOWN, 3),
    ("send", "-", UP, 3), ("send", "-", XOWN, 2), ("send", "-", XOWN, 3),
    ("mul", 0, 256, (FAR,)),
    ("got", FAR, 2),
    ("send", "x", FAR, 2),
    ("mul", 384, 128, (UP, DOWN, XOWN)),
    ("got", XUP, 0), ("got", XDOWN, 0), ("got", XFAR, 0),
    ("mul", 0, 128, (XUP, XDOWN, XFAR)),
    ("got", FAR, 3),
    ("send", "x", FAR, 3),
    ("got", XUP, 1), ("got", XDOWN, 1), ("got", XFAR, 1),
    ("finish", 0),
    ("mul", 128, 128, (XUP, XDOWN, XFAR)),
    ("mul", 256, 256, (FAR,)),
    ("got", XUP, 2), ("got", XDOWN, 2), ("got", XFAR, 2),
    ("finish", 1),
    ("mul", 256, 128, (XUP, XDOWN, XFAR)),
    ("got", XUP, 3), ("got", XDOWN, 3), ("got", XFAR, 3),
    ("finish", 2),
    ("mul", 384, 128, (XUP, XDOWN, XFAR)),
    ("finish", 3),
]

SENDS = [step[1:] for step in PROGRAM if step[0] == "send"]
ARRIVALS = {(seen_by(c, link), q): i for i, (link, c, q) in enumerate(SENDS)}
assert len(ARRIVALS) == len(SENDS) == 28

W_ORDER = [OWN, UP, DOWN, XOWN, FAR, XUP, XDOWN, XFAR]


def kernel(
    hidden, weights, sampled, bits,
    full_out, kept_out, mean_out,
    h, w, acc, ids_flat, bits_flat, ids, keeps, top, ktop, total, ktotal, taken,
    stats, gaps,
    load_sem, w_sem, send_sem, recv_sem, share_send, share_recv,
    stat_send, stat_recv, gap_send, gap_recv,
):
    v = lax.axis_index("vocab")
    r = lax.axis_index("rows")
    core = lax.rem(v, 2)
    chip = v // 2
    xh = chip // 4
    y = lax.rem(chip, 4)
    sibling = v + 1 - 2 * core
    mine = pl.ds(pl.multiple_of(core * FEAT, FEAT), FEAT)
    slot = {
        (dx, dy): lax.rem(xh + dx, 2) * 4 + lax.rem(y + dy, 4)
        for dx in range(2)
        for dy in range(4)
    }
    target = {link: slot[d] * 2 + core for link, d in LINKS.items()}

    own_load = pltpu.make_async_copy(hidden, h.at[chip, :, mine], load_sem.at[0])
    own_load.start()
    ids_load = pltpu.make_async_copy(sampled, ids_flat, load_sem.at[1])
    ids_load.start()
    bits_load = pltpu.make_async_copy(bits, bits_flat, load_sem.at[2])
    bits_load.start()
    w_loads = {}
    for i, c in enumerate(W_ORDER):
        rows = pl.ds(pl.multiple_of(slot[c] * CHIP_FEAT, CHIP_FEAT), CHIP_FEAT)
        w_loads[c] = pltpu.make_async_copy(weights.at[rows, :], w.at[slot[c]], w_sem.at[i])
        w_loads[c].start()

    barrier = pltpu.get_barrier_semaphore()
    peers = [lax.rem(v + i, N_VOCAB) for i in range(1, N_VOCAB)]
    row_peers = [lax.rem(r + i, N_ROWS) for i in range(1, N_ROWS)]
    for p in peers:
        pl.semaphore_signal(barrier, inc=1, device_id={"vocab": p}, device_id_type=MESH)
    for p in row_peers:
        pl.semaphore_signal(barrier, inc=1, device_id={"rows": p}, device_id_type=MESH)
    pl.semaphore_wait(barrier, len(peers) + len(row_peers))

    started = []

    def send(i, link, c, q):
        rows = pl.ds(q * Q, Q)
        src = hidden.at[rows, :] if c == OWN else h.at[slot[c], rows, mine]
        copy = pltpu.make_async_remote_copy(
            src_ref=src,
            dst_ref=h.at[slot[c], rows, mine],
            send_sem=send_sem.at[i],
            recv_sem=recv_sem.at[i],
            device_id={"vocab": target[link]},
            device_id_type=MESH,
        )
        copy.start()
        started.append(copy)

    def arrival(i, c, q):
        part = h.at[slot[c], pl.ds(q * Q, Q), mine]
        return pltpu.make_async_remote_copy(
            src_ref=part, dst_ref=part, send_sem=send_sem.at[i], recv_sem=recv_sem.at[i],
            device_id={"vocab": sibling}, device_id_type=MESH,
        )

    def share(i, c, q):
        part = h.at[slot[c], pl.ds(q * Q, Q), mine]
        copy = pltpu.make_async_remote_copy(
            src_ref=part, dst_ref=part, send_sem=share_send.at[i], recv_sem=share_recv.at[i],
            device_id={"vocab": sibling}, device_id_type=MESH,
        )
        copy.start()
        started.append(copy)
        return copy

    shared = {}
    ready_w = set()

    def product(r0, size, chunks, first=False):
        for c in chunks:
            if c not in ready_w:
                w_loads[c].wait()
                ready_w.add(c)
            if c != OWN:
                for q in range(r0 // Q, (r0 + size) // Q):
                    shared[c, q].wait_recv()
        rows = slice(r0, r0 + size)
        for j in range(0, WIDTH, TILE):
            cols = slice(j, min(j + TILE, WIDTH))
            t = None
            for c in chunks:
                d = jnp.dot(h[slot[c], rows, :], w[slot[c], :, cols], preferred_element_type=F32)
                t = d if t is None else t + d
            acc[rows, cols] = t if first else acc[rows, cols] + t

    def finish(q):
        group = 32

        def part(g, _):
            rows = pl.ds(pl.multiple_of(q * Q + g * group, group), group)
            here = pl.ds(pl.multiple_of(g * group, group), group)
            kept_bits = keeps[rows, :]
            token = ids[rows, :] - v * WIDTH - lax.broadcasted_iota(jnp.int32, (group, VBLK), 1)
            m = km = pk = None
            for b in range(NBLK):
                z = acc[rows, b * VBLK:(b + 1) * VBLK]
                kz = jnp.where((kept_bits & (1 << b)) != 0, z, ABSENT)
                hit = jnp.where(token == b * VBLK, z, 0.0)
                m = z if m is None else jnp.maximum(m, z)
                km = kz if km is None else jnp.maximum(km, kz)
                pk = hit if pk is None else pk + hit
            s = jnp.zeros((group, VBLK), F32)
            ks = jnp.zeros((group, VBLK), F32)
            for b in range(NBLK):
                z = acc[rows, b * VBLK:(b + 1) * VBLK]
                kz = jnp.where((kept_bits & (1 << b)) != 0, z, ABSENT)
                s += jnp.exp2((z - m) * EXP_SCALE)
                ks += jnp.exp2((kz - km) * EXP_SCALE)
            top[here, :] = m
            ktop[here, :] = km
            total[here, :] = s
            ktotal[here, :] = ks
            taken[here, :] = pk
            return 0

        lax.fori_loop(0, Q // group, part, 0)

        def combined(maxes, sums):
            mt = maxes[...].T
            st = sums[...].T
            best = jnp.max(mt, axis=0, keepdims=True)
            whole = jnp.sum(st * jnp.exp2((mt - best) * EXP_SCALE), axis=0, keepdims=True)
            return best / SOFTNESS + jnp.log(whole)

        full = combined(top, total)
        kept = combined(ktop, ktotal)
        picked = jnp.sum(taken[...].T, axis=0, keepdims=True) / SOFTNESS
        stats[v, q, 0:1, :] = full
        stats[v, q, 1:2, :] = kept
        stats[v, q, 2:3, :] = picked
        stats[v, q, 3:4, :] = picked
        for i, p in enumerate(peers):
            copy = pltpu.make_async_remote_copy(
                src_ref=stats.at[v, q], dst_ref=stats.at[v, q],
                send_sem=stat_send.at[q, i], recv_sem=stat_recv.at[q, i],
                device_id={"vocab": p}, device_id_type=MESH,
            )
            copy.start()
            started.append(copy)
            stat_copies[q].append(copy)

    def conclude(q):
        for copy in stat_copies[q]:
            copy.wait_recv()
        best = stats[0, q]
        for i in range(1, N_VOCAB):
            best = jnp.maximum(best, stats[i, q])
        whole = jnp.zeros((4, Q), F32)
        chosen = jnp.zeros((4, Q), F32)
        for i in range(N_VOCAB):
            s = stats[i, q]
            whole += jnp.exp(s - best)
            chosen += s
        lse = best + jnp.log(whole)
        picked = chosen[2:3]
        full = picked - lse[0:1]
        kept = picked - lse[1:2]
        full_out[q:q + 1, :] = full
        kept_out[q:q + 1, :] = kept
        return kept - full

    stat_copies = [[] for _ in range(NQ)]

    ids_load.wait()
    bits_load.wait()

    sent = 0
    for step in PROGRAM:
        if step[0] == "send":
            send(sent, *step[1:])
            sent += 1
        elif step[0] == "own":
            own = pltpu.make_async_remote_copy(
                src_ref=hidden, dst_ref=h.at[chip, :, mine],
                send_sem=share_send.at[28], recv_sem=share_recv.at[28],
                device_id={"vocab": sibling}, device_id_type=MESH,
            )
            own.start()
            started.append(own)
            for q in range(NQ):
                rows = slice(q * Q, (q + 1) * Q)
                ids[rows, :] = jnp.broadcast_to(ids_flat[q:q + 1, :], (VBLK, Q)).T
                keeps[rows, :] = jnp.broadcast_to(bits_flat[q:q + 1, :], (VBLK, Q)).T
            own_load.wait()
            own.wait_recv()
            product(0, ROWS, (OWN,), first=True)
        elif step[0] == "got":
            i = ARRIVALS[step[1:]]
            arrival(i, *step[1:]).wait_recv()
            shared[step[1:]] = share(i, *step[1:])
        elif step[0] == "mul":
            product(*step[1:])
        else:
            finish(step[1])

    gap = None
    for q in range(NQ):
        g = conclude(q)
        gap = g if gap is None else gap + g
    gaps[r] = jnp.broadcast_to(gap, (8, Q))
    gap_copies = []
    for i, p in enumerate(row_peers):
        copy = pltpu.make_async_remote_copy(
            src_ref=gaps.at[r], dst_ref=gaps.at[r],
            send_sem=gap_send.at[i], recv_sem=gap_recv.at[i],
            device_id={"rows": p}, device_id_type=MESH,
        )
        copy.start()
        started.append(copy)
        gap_copies.append(copy)
    for copy in started:
        copy.wait_send()
    for copy in gap_copies:
        copy.wait_recv()
    everything = gaps[0]
    for i in range(1, N_ROWS):
        everything += gaps[i]
    mean_out[...] = jnp.sum(everything[0:1], axis=1, keepdims=True) / TOKENS


def per_device(hidden, weights, sampled, keep_bits):
    anywhere = pl.BlockSpec(memory_space=pl.ANY)
    vmem = pl.BlockSpec(memory_space=pltpu.VMEM)
    dma = pltpu.SemaphoreType.DMA
    full, kept, mean = pl.pallas_call(
        kernel,
        out_shape=(
            jax.ShapeDtypeStruct((NQ, Q), F32),
            jax.ShapeDtypeStruct((NQ, Q), F32),
            jax.ShapeDtypeStruct((1, 1), F32),
        ),
        in_specs=[anywhere] * 4,
        out_specs=(vmem, vmem, vmem),
        scratch_shapes=[
            pltpu.VMEM((CHIPS, ROWS, CHIP_FEAT), jnp.bfloat16),
            pltpu.VMEM((CHIPS, CHIP_FEAT, WIDTH), jnp.bfloat16),
            pltpu.VMEM((ROWS, WIDTH), F32),
            pltpu.VMEM((NQ, Q), jnp.int32),
            pltpu.VMEM((NQ, Q), jnp.int32),
            pltpu.VMEM((ROWS, VBLK), jnp.int32),
            pltpu.VMEM((ROWS, VBLK), jnp.int32),
            pltpu.VMEM((Q, VBLK), F32),
            pltpu.VMEM((Q, VBLK), F32),
            pltpu.VMEM((Q, VBLK), F32),
            pltpu.VMEM((Q, VBLK), F32),
            pltpu.VMEM((Q, VBLK), F32),
            pltpu.VMEM((N_VOCAB, NQ, 4, Q), F32),
            pltpu.VMEM((N_ROWS, 8, Q), F32),
            dma((3,)),
            dma((CHIPS,)),
            dma((28,)),
            dma((28,)),
            dma((29,)),
            dma((29,)),
            dma((NQ, N_VOCAB - 1)),
            dma((NQ, N_VOCAB - 1)),
            dma((N_ROWS - 1,)),
            dma((N_ROWS - 1,)),
        ],
        compiler_params=pltpu.CompilerParams(
            collective_id=0, has_side_effects=True, vmem_limit_bytes=56 << 20
        ),
        cost_estimate=pl.CostEstimate(
            flops=2 * ROWS * WIDTH * CHIPS * CHIP_FEAT,
            bytes_accessed=2 * CHIPS * CHIP_FEAT * WIDTH,
            transcendentals=2 * ROWS * WIDTH,
        ),
    )(hidden, weights, sampled.reshape(NQ, Q), keep_bits.reshape(NQ, Q))
    return full.reshape(ROWS), kept.reshape(ROWS), mean.reshape(())


def solution(mesh):
    placed = (P("rows", "vocab"), P(None, "vocab"), P("rows"), P("rows", "vocab"))
    return jax.shard_map(
        per_device,
        mesh=mesh,
        in_specs=placed,
        out_specs=(P("rows"), P("rows"), P()),
        check_vma=False,
    )
```

time: 190 us -> 53.1 us (0.28); the launches traced: 187 us -> 52.9 us
  blocking collectives: 83.8 us -> 0 us
  waiting for transfers between devices: 60.2 us -> 0 us
  Pallas kernels: 0 us -> 48 us
  matrix products: 18.6 us -> 0 us
  between operations: 15.8 us -> 2.4 us
  other arithmetic: 7.02 us -> 0 us
    all_gather x1 -> x0, waiting for transfers between devices: 59.5 us -> none  [per_device(): whole = lax.all_gather(hidden, 'vocab', axis=1, tiled=True)]
    psum x2 -> x0, blocking collectives: 51 us -> none  [the longest x1 34.3 us: per_device(): lax.psum((full_sum, kept_sum, picked), 'vocab')]
    pallas_call x0 -> x1, Pallas kernels: none -> 48 us  [per_device(): pl.pallas_call(kernel, out_shape=(jax.ShapeDtypeStruct((NQ, Q), F32), jax...]
    pmax x1 -> x0, blocking collectives: 32.8 us -> none  [per_device(): full_max, kept_max = lax.pmax((full_top, kept_top), 'vocab')]
    dot_general x1 -> x0, matrix products: 18.6 us -> none  [per_device(): jnp.dot(whole, lexicon_projection_weights, preferred_element_type=jnp.flo...]
    reduce_sum x2 -> x0, other arithmetic: 5.64 us -> none  [the longest x1 4.45 us: per_device(): jnp.sum(jnp.where(is_kept, jnp.exp(raw_preference_values - kept_max[:, No...]
    unnamed x0 -> x2, local copies, waits for them, and re-layouts: none -> 2.48 us
  transfers between devices with their start and end apart: 1 -> 0, of which waited for: 1 -> 0; matrix products, arithmetic and copies ran while one was open for 2% -> 0% of each run, Pallas kernels for 0% -> 0%
where the time goes in v1:
time: 53.1 us; the launch traced here: 52.9 us
  Pallas kernels  48 us (90%)
  local copies, waits for them, and re-layouts  2.48 us (5%)
  between operations  2.4 us (5%)
    pallas_call x1, Pallas kernels, per_device(): pl.pallas_call(kernel, out_shape=(jax.ShapeDtypeStruct((NQ, Q), F32), jax...  48 us
    unnamed x2, local copies, waits for them, and re-layouts  2.48 us

profile of v1, /device:TPU:1, one launch (start us, length us, event | category | flops | bytes accessed | tf_op | source)
XLA Modules:
  0.0 52.9 jit_solution(10515483678647455536)
XLA Ops:
  0.6 48.0 %shard_map.67 = (f32[4,128]{1,0:T(4,128)}, f32[4,128]{1,0:T(4,128)}, f32[1,1]{1,0:T(1,128)}) custom-call(bf16[512,256]{1,0:T(8,128)(2,1)} %hidden.1, bf16[4096,2432]{1,0:T(8,128)(2,1)} %weights.1, s32[4,128]{1,0:T(4,128)} %bitcast.7, s32[4,128]{1,0:T(4,128)} %bitcast.8), custom_call_target="tpu_custom_call" | custom-call | flops 10200547328 | bytes 19922944 | tf_op jit(solution)/shard_map/pallas_call | solution.py:326
  48.6 1.2 %copy.10 = f32[512]{0:T(512)} copy(f32[512]{0:T(512)} %bitcast.6) | data formatting | bytes 4096
  49.9 1.2 %copy.11 = f32[512]{0:T(512)} copy(f32[512]{0:T(512)} %bitcast.5) | data formatting | bytes 4096

commit v2 on v1

v2 whole, which is shorter than its diff:
```python
import jax
import jax.numpy as jnp
from jax import lax
from jax.experimental import pallas as pl
from jax.experimental.pallas import tpu as pltpu
from jax.sharding import PartitionSpec as P

MESH = pl.DeviceIdType.MESH
F32 = jnp.float32

SOFTNESS = 0.7
LOG2E = 1.4426950408889634
EXP_SCALE = LOG2E / SOFTNESS
ABSENT = -2.3819e38

TOKENS = 4096
ROWS = 512
FEAT = 256
CHIP_FEAT = 512
CHIPS = 8
WIDTH = 2432
VBLK = 128
NBLK = 19
TILE = 256
Q = 128
NQ = 4
N_VOCAB = 16
N_ROWS = 8

OWN, UP, DOWN, FAR = (0, 0), (0, 1), (0, 3), (0, 2)
XOWN, XUP, XDOWN, XFAR = (1, 0), (1, 1), (1, 3), (1, 2)

LINKS = {"+": (0, 1), "-": (0, 3), "x": (1, 0)}


def seen_by(chunk, link):
    dx, dy = LINKS[link]
    return ((chunk[0] + dx) % 2, (chunk[1] - dy) % 4)


NEAR = (UP, DOWN, XOWN)
CROSS = (XUP, XDOWN, XFAR)


def at(chunks, r0, n=Q):
    return tuple((c, r0, n) for c in chunks)


PROGRAM = [
    ("send", "+", OWN, 0, 128), ("send", "-", OWN, 256, 128), ("send", "x", OWN, 0, 128),
    ("send", "+", OWN, 128, 128), ("send", "-", OWN, 384, 128), ("send", "x", OWN, 128, 128),
    ("send", "+", OWN, 256, 128), ("send", "-", OWN, 0, 128), ("send", "x", OWN, 256, 128),
    ("send", "x", OWN, 384, 128),
    ("own",),
    ("got", ((DOWN, 0, 128), (UP, 256, 128))),
    ("send", "+", DOWN, 0, 128), ("send", "-", UP, 256, 128),
    ("send", "+", OWN, 384, 128), ("send", "-", OWN, 128, 128),
    ("got", ((XOWN, 0, 128),)),
    ("got", ((DOWN, 128, 128), (UP, 384, 128))),
    ("send", "+", DOWN, 128, 128), ("send", "-", UP, 384, 128),
    ("send", "+", XOWN, 0, 128), ("send", "-", XOWN, 0, 128),
    ("mul", 0, 128, (DOWN, XOWN)),
    ("got", ((XOWN, 128, 128),)),
    ("got", ((DOWN, 256, 128), (UP, 0, 128))),
    ("mul", 128, 128, (DOWN, XOWN)),
    ("mul", 256, 256, (UP,)),
    ("got", ((FAR, 0, 128), (FAR, 256, 128))),
    ("send", "x", FAR, 0, 128), ("send", "x", FAR, 256, 128),
    ("got", ((XOWN, 256, 128), (XOWN, 384, 128))),
    ("send", "+", XOWN, 256, 128), ("send", "-", XOWN, 256, 128),
    ("send", "+", XOWN, 128, 128), ("send", "-", XOWN, 128, 128),
    ("send", "+", XOWN, 384, 128), ("send", "-", XOWN, 384, 128),
    ("mul", 256, 128, (DOWN, XOWN)),
    ("got", ((DOWN, 384, 128), (UP, 128, 128))),
    ("mul", 384, 128, (DOWN, XOWN)),
    ("got", ((FAR, 128, 128), (FAR, 384, 128))),
    ("send", "x", FAR, 128, 128), ("send", "x", FAR, 384, 128),
    ("mul", 0, 256, (UP,)),
    ("got", at(CROSS, 0)),
    ("mul", 0, 512, (FAR,)),
    ("got", at(CROSS, 256)),
    ("last", 0),
    ("got", at(CROSS, 128)),
    ("last", 2),
    ("got", at(CROSS, 384)),
    ("last", 1),
    ("last", 3),
]

SENDS = [step[1:] for step in PROGRAM if step[0] == "send"]
GROUPS = [step[1] for step in PROGRAM if step[0] == "got"]
GROUP_OF = {piece: i for i, group in enumerate(GROUPS) for piece in group}
assert {(seen_by(c, link), r0, n) for link, c, r0, n in SENDS} == set(GROUP_OF)
SENT_ROWS = sum(n for _, _, _, n in SENDS)
assert SENT_ROWS == 7 * ROWS

W_ORDER = [OWN, UP, DOWN, XOWN, FAR, XUP, XDOWN, XFAR]


def kernel(
    hidden, weights, sampled, bits,
    out,
    h, w, acc, kacc, ids_flat, bits_flat, ids, keeps, top, ktop, total, ktotal, taken,
    stats, gaps,
    load_sem, w_sem, send_sem, recv_sem, share_recv,
    stat_send, stat_recv, gap_send, gap_recv,
):
    v = lax.axis_index("vocab")
    r = lax.axis_index("rows")
    core = lax.rem(v, 2)
    chip = v // 2
    xh = chip // 4
    y = lax.rem(chip, 4)
    sibling = v + 1 - 2 * core
    mine = pl.ds(pl.multiple_of(core * FEAT, FEAT), FEAT)
    slot = {
        (dx, dy): lax.rem(xh + dx, 2) * 4 + lax.rem(y + dy, 4)
        for dx in range(2)
        for dy in range(4)
    }
    target = {link: slot[d] * 2 + core for link, d in LINKS.items()}

    own_load = pltpu.make_async_copy(hidden, h.at[chip, :, mine], load_sem.at[0])
    own_load.start()
    ids_load = pltpu.make_async_copy(sampled, ids_flat, load_sem.at[1])
    ids_load.start()
    bits_load = pltpu.make_async_copy(bits, bits_flat, load_sem.at[2])
    bits_load.start()
    w_loads = {}
    for i, c in enumerate(W_ORDER):
        rows = pl.ds(pl.multiple_of(slot[c] * CHIP_FEAT, CHIP_FEAT), CHIP_FEAT)
        w_loads[c] = pltpu.make_async_copy(weights.at[rows, :], w.at[slot[c]], w_sem.at[i])
        if c == OWN:
            w_loads[c].start()

    barrier = pltpu.get_barrier_semaphore()
    peers = [lax.rem(v + i, N_VOCAB) for i in range(1, N_VOCAB)]
    row_peers = [lax.rem(r + i, N_ROWS) for i in range(1, N_ROWS)]
    for p in peers:
        pl.semaphore_signal(barrier, inc=1, device_id={"vocab": p}, device_id_type=MESH)
    for p in row_peers:
        pl.semaphore_signal(barrier, inc=1, device_id={"rows": p}, device_id_type=MESH)
    pl.semaphore_wait(barrier, len(peers) + len(row_peers))

    def send(link, c, r0, n):
        rows = pl.ds(r0, n)
        src = h.at[slot[c], rows, mine]
        pltpu.make_async_remote_copy(
            src_ref=src,
            dst_ref=h.at[slot[c], rows, mine],
            send_sem=send_sem,
            recv_sem=recv_sem.at[GROUP_OF[seen_by(c, link), r0, n]],
            device_id={"vocab": target[link]},
            device_id_type=MESH,
        ).start()

    def wait_rows(n, sem):
        part = h.at[0, pl.ds(0, n), mine]
        pltpu.make_async_copy(part, part, sem).wait()

    def share(src, dst, i):
        pltpu.make_async_remote_copy(
            src_ref=src, dst_ref=dst, send_sem=send_sem, recv_sem=share_recv.at[i],
            device_id={"vocab": sibling}, device_id_type=MESH,
        ).start()

    shared = set()
    ready_w = set()

    def need(group):
        if group not in shared:
            shared.add(group)
            wait_rows(sum(n for _, _, n in GROUPS[group]), share_recv.at[group])

    def product(r0, size, chunks, first=False, seen=None):
        for c in chunks:
            if c not in ready_w:
                w_loads[c].wait()
                ready_w.add(c)
            if c != OWN:
                for (pc, p0, n), group in GROUP_OF.items():
                    if pc == c and p0 < r0 + size and r0 < p0 + n:
                        need(group)
        rows = slice(r0, r0 + size)
        for j in range(0, WIDTH, TILE):
            cols = slice(j, min(j + TILE, WIDTH))
            t = None
            for c in chunks:
                d = jnp.dot(h[slot[c], rows, :], w[slot[c], :, cols], preferred_element_type=F32)
                t = d if t is None else t + d
            t = t if first else acc[rows, cols] + t
            acc[rows, cols] = t
            if seen is not None:
                seen(rows, cols.start, t)

    def finish(q):
        mine_q = slice(q * Q, (q + 1) * Q)
        token = ids[mine_q, :]
        kept_bits = keeps[mine_q, :]

        def seen(rows, c0, t):
            for i in range(t.shape[1] // VBLK):
                b = c0 // VBLK + i
                z = t[:, i * VBLK:(i + 1) * VBLK]
                kz = jnp.where((kept_bits & (1 << b)) != 0, z, ABSENT)
                hit = jnp.where(token == b * VBLK, z, 0.0)
                kacc[:, b * VBLK:(b + 1) * VBLK] = kz
                top[...] = z if b == 0 else jnp.maximum(top[...], z)
                ktop[...] = kz if b == 0 else jnp.maximum(ktop[...], kz)
                taken[...] = hit if b == 0 else taken[...] + hit

        product(q * Q, Q, CROSS, seen=seen)
        group = 32

        def part(g, _):
            rows = pl.ds(pl.multiple_of(q * Q + g * group, group), group)
            here = pl.ds(pl.multiple_of(g * group, group), group)
            m = top[here, :]
            km = ktop[here, :]
            s = jnp.zeros((group, VBLK), F32)
            ks = jnp.zeros((group, VBLK), F32)
            for b in range(NBLK):
                cols = slice(b * VBLK, (b + 1) * VBLK)
                s += jnp.exp2((acc[rows, cols] - m) * EXP_SCALE)
                ks += jnp.exp2((kacc[here, cols] - km) * EXP_SCALE)
            total[here, :] = s
            ktotal[here, :] = ks
            return 0

        lax.fori_loop(0, Q // group, part, 0)

        def combined(maxes, sums):
            mt = maxes[...].T
            st = sums[...].T
            best = jnp.max(mt, axis=0, keepdims=True)
            whole = jnp.sum(st * jnp.exp2((mt - best) * EXP_SCALE), axis=0, keepdims=True)
            return best / SOFTNESS + jnp.log(whole)

        full = combined(top, total)
        kept = combined(ktop, ktotal)
        picked = jnp.sum(taken[...].T, axis=0, keepdims=True) / SOFTNESS
        stats[q, v, 0:1, :] = full
        stats[q, v, 1:2, :] = kept
        stats[q, v, 2:3, :] = picked
        stats[q, v, 3:4, :] = picked
        for p in peers:
            pltpu.make_async_remote_copy(
                src_ref=stats.at[q, v], dst_ref=stats.at[q, v],
                send_sem=stat_send, recv_sem=stat_recv.at[q],
                device_id={"vocab": p}, device_id_type=MESH,
            ).start()

    def conclude(q):
        others = stats.at[q, 0:N_VOCAB - 1]
        pltpu.make_async_copy(others, others, stat_recv.at[q]).wait()
        best = stats[q, 0]
        for i in range(1, N_VOCAB):
            best = jnp.maximum(best, stats[q, i])
        whole = jnp.zeros((4, Q), F32)
        chosen = jnp.zeros((4, Q), F32)
        for i in range(N_VOCAB):
            s = stats[q, i]
            whole += jnp.exp(s - best)
            chosen += s
        lse = best + jnp.log(whole)
        picked = chosen[2:3]
        full = picked - lse[0:1]
        kept = picked - lse[1:2]
        out[q:q + 1, :] = full
        out[NQ + q:NQ + q + 1, :] = kept
        return kept - full

    own_load.wait()
    ids_load.wait()
    bits_load.wait()

    for step in PROGRAM:
        if step[0] == "send":
            send(*step[1:])
        elif step[0] == "own":
            for c in W_ORDER[1:]:
                w_loads[c].start()
            share(h.at[chip, :, mine], h.at[chip, :, mine], len(GROUPS))
            for q in range(NQ):
                rows = slice(q * Q, (q + 1) * Q)
                lanes = lax.broadcasted_iota(jnp.int32, (Q, VBLK), 1) + v * WIDTH
                ids[rows, :] = jnp.broadcast_to(ids_flat[q:q + 1, :], (VBLK, Q)).T - lanes
                keeps[rows, :] = jnp.broadcast_to(bits_flat[q:q + 1, :], (VBLK, Q)).T
            wait_rows(ROWS, share_recv.at[len(GROUPS)])
            product(0, ROWS, (OWN,), first=True)
        elif step[0] == "got":
            group = GROUP_OF[step[1][0]]
            wait_rows(sum(n for _, _, n in step[1]), recv_sem.at[group])
            for c, r0, n in step[1]:
                part = h.at[slot[c], pl.ds(r0, n), mine]
                share(part, part, group)
        elif step[0] == "mul":
            product(*step[1:])
        else:
            finish(step[1])

    gap = None
    for q in range(NQ):
        g = conclude(q)
        gap = g if gap is None else gap + g
    gaps[r] = jnp.broadcast_to(gap, (8, Q))
    for p in row_peers:
        pltpu.make_async_remote_copy(
            src_ref=gaps.at[r], dst_ref=gaps.at[r],
            send_sem=gap_send, recv_sem=gap_recv,
            device_id={"rows": p}, device_id_type=MESH,
        ).start()
    everyone = h.at[:, pl.ds(0, ROWS * 15 // 16), :]
    pltpu.make_async_copy(everyone, everyone, send_sem).wait()
    whole_stats = stats.at[:, 0:N_VOCAB - 1]
    pltpu.make_async_copy(whole_stats, whole_stats, stat_send).wait()
    others = gaps.at[0:N_ROWS - 1]
    pltpu.make_async_copy(others, others, gap_recv).wait()
    everything = gaps[0]
    for i in range(1, N_ROWS):
        everything += gaps[i]
    mean = jnp.sum(everything[0:1], axis=1, keepdims=True) / TOKENS
    out[2 * NQ:2 * NQ + 1, :] = jnp.broadcast_to(mean, (1, Q))
    pltpu.make_async_copy(others, others, gap_send).wait()


def per_device(hidden, weights, sampled, keep_bits):
    anywhere = pl.BlockSpec(memory_space=pl.ANY)
    vmem = pl.BlockSpec(memory_space=pltpu.VMEM)
    dma = pltpu.SemaphoreType.DMA
    out = pl.pallas_call(
        kernel,
        out_shape=jax.ShapeDtypeStruct((2 * NQ + 1, Q), F32),
        in_specs=[anywhere] * 4,
        out_specs=vmem,
        scratch_shapes=[
            pltpu.VMEM((CHIPS, ROWS, CHIP_FEAT), jnp.bfloat16),
            pltpu.VMEM((CHIPS, CHIP_FEAT, WIDTH), jnp.bfloat16),
            pltpu.VMEM((ROWS, WIDTH), F32),
            pltpu.VMEM((Q, WIDTH), F32),
            pltpu.VMEM((NQ, Q), jnp.int32),
            pltpu.VMEM((NQ, Q), jnp.int32),
            pltpu.VMEM((ROWS, VBLK), jnp.int32),
            pltpu.VMEM((ROWS, VBLK), jnp.int32),
            pltpu.VMEM((Q, VBLK), F32),
            pltpu.VMEM((Q, VBLK), F32),
            pltpu.VMEM((Q, VBLK), F32),
            pltpu.VMEM((Q, VBLK), F32),
            pltpu.VMEM((Q, VBLK), F32),
            pltpu.VMEM((NQ, N_VOCAB, 4, Q), F32),
            pltpu.VMEM((N_ROWS, 8, Q), F32),
            dma((3,)),
            dma((CHIPS,)),
            dma,
            dma((len(GROUPS),)),
            dma((len(GROUPS) + 1,)),
            dma,
            dma((NQ,)),
            dma,
            dma,
        ],
        compiler_params=pltpu.CompilerParams(
            collective_id=0, has_side_effects=True, vmem_limit_bytes=56 << 20
        ),
        cost_estimate=pl.CostEstimate(
            flops=2 * ROWS * WIDTH * CHIPS * CHIP_FEAT,
            bytes_accessed=2 * CHIPS * CHIP_FEAT * WIDTH,
            transcendentals=2 * ROWS * WIDTH,
        ),
    )(hidden, weights, sampled.reshape(NQ, Q), keep_bits.reshape(NQ, Q))
    return out[:NQ].reshape(ROWS), out[NQ:2 * NQ].reshape(ROWS), out[2 * NQ, 0]


def solution(mesh):
    placed = (P("rows", "vocab"), P(None, "vocab"), P("rows"), P("rows", "vocab"))
    return jax.shard_map(
        per_device,
        mesh=mesh,
        in_specs=placed,
        out_specs=(P("rows"), P("rows"), P()),
        check_vma=False,
    )
```

time: 53.1 us -> 44.9 us (0.85)
  Pallas kernels: 48 us -> 41.6 us
  between operations: 2.4 us -> 0.64 us
    pallas_call x1, Pallas kernels: 48 us -> 41.6 us  [per_device(): pl.pallas_call(kernel, out_shape=jax.ShapeDtypeStruct((2 * NQ + 1, Q), F3...]
    unnamed x2 -> x0, local copies, waits for them, and re-layouts: 2.48 us -> none
    reshape x0 -> x1, local copies, waits for them, and re-layouts: none -> 1.33 us  [per_device(): out[NQ:2 * NQ].reshape(ROWS)]
    slice x0 -> x1, local copies, waits for them, and re-layouts: none -> 1.19 us  [per_device(): out[2 * NQ, 0]]
where the time goes in v2:
time: 44.9 us; the launch traced here: 44.7 us
  Pallas kernels  41.6 us (93%)
  local copies, waits for them, and re-layouts  2.52 us (6%)
  between operations  0.64 us (1%)
    pallas_call x1, Pallas kernels, per_device(): pl.pallas_call(kernel, out_shape=jax.ShapeDtypeStruct((2 * NQ + 1, Q), F3...  41.6 us
    reshape x1, local copies, waits for them, and re-layouts, per_device(): out[NQ:2 * NQ].reshape(ROWS)  1.33 us
    slice x1, local copies, waits for them, and re-layouts, per_device(): out[2 * NQ, 0]  1.19 us

profile of v2, /device:TPU:1, one launch (start us, length us, event | category | flops | bytes accessed | tf_op | source)
XLA Modules:
  0.0 44.7 jit_solution(10201071427371589310)
XLA Ops:
  0.6 41.6 %shard_map.67 = f32[9,128]{1,0:T(8,128)} custom-call(bf16[512,256]{1,0:T(8,128)(2,1)} %hidden.1, bf16[4096,2432]{1,0:T(8,128)(2,1)} %weights.1, s32[4,128]{1,0:T(4,128)} %bitcast.7, s32[4,128]{1,0:T(4,128)} %bitcast.8), custom_call_target="tpu_custom_call" | custom-call | flops 10200547328 | bytes 19922944 | tf_op jit(solution)/shard_map/pallas_call | solution.py:331
  42.2 1.3 %slice_bitcast_fusion = (f32[512]{0:T(512)}, f32[512]{0:T(512)}) fusion(f32[9,128]{1,0:T(8,128)} %shard_map.67), kind=kLoop, calls=%fused_computation | loop fusion | bytes 8192 | tf_op jit(solution)/shard_map/reshape | solution.py:371
  43.5 1.2 %slice.11 = f32[1,1]{1,0:T(1,128)} slice(f32[9,128]{1,0:T(8,128)} %shard_map.67), slice={[8:9], [0:1]} | slice | bytes 8 | tf_op jit(solution)/shard_map/slice | solution.py:371

commit v3 on v2

--- a/solution.py
+++ b/solution.py
@@ -1,3 +1,5 @@
+import functools
+
 import jax
 import jax.numpy as jnp
 from jax import lax
@@ -63,21 +65,22 @@
     ("got", ((XOWN, 128, 128),)),
     ("got", ((DOWN, 256, 128), (UP, 0, 128))),
     ("mul", 128, 128, (DOWN, XOWN)),
-    ("mul", 256, 256, (UP,)),
     ("got", ((FAR, 0, 128), (FAR, 256, 128))),
     ("send", "x", FAR, 0, 128), ("send", "x", FAR, 256, 128),
+    ("mul", 256, 256, (UP,)),
     ("got", ((XOWN, 256, 128), (XOWN, 384, 128))),
     ("send", "+", XOWN, 256, 128), ("send", "-", XOWN, 256, 128),
     ("send", "+", XOWN, 128, 128), ("send", "-", XOWN, 128, 128),
     ("send", "+", XOWN, 384, 128), ("send", "-", XOWN, 384, 128),
     ("mul", 256, 128, (DOWN, XOWN)),
     ("got", ((DOWN, 384, 128), (UP, 128, 128))),
-    ("mul", 384, 128, (DOWN, XOWN)),
     ("got", ((FAR, 128, 128), (FAR, 384, 128))),
     ("send", "x", FAR, 128, 128), ("send", "x", FAR, 384, 128),
+    ("mul", 384, 128, (DOWN, XOWN)),
     ("mul", 0, 256, (UP,)),
+    ("mul", 0, 256, (FAR,)),
     ("got", at(CROSS, 0)),
-    ("mul", 0, 512, (FAR,)),
+    ("mul", 256, 256, (FAR,)),
     ("got", at(CROSS, 256)),
     ("last", 0),
     ("got", at(CROSS, 128)),
@@ -120,6 +123,14 @@
     }
     target = {link: slot[d] * 2 + core for link, d in LINKS.items()}
 
+    barrier = pltpu.get_barrier_semaphore()
+    peers = [lax.rem(v + i, N_VOCAB) for i in range(1, N_VOCAB)]
+    row_peers = [lax.rem(r + i, N_ROWS) for i in range(1, N_ROWS)]
+    for p in (target["+"], target["-"], target["x"], sibling):
+        pl.semaphore_signal(barrier, inc=1, device_id={"vocab": p}, device_id_type=MESH)
+    for p in row_peers:
+        pl.semaphore_signal(barrier, inc=1, device_id={"rows": p}, device_id_type=MESH)
+
     own_load = pltpu.make_async_copy(hidden, h.at[chip, :, mine], load_sem.at[0])
     own_load.start()
     ids_load = pltpu.make_async_copy(sampled, ids_flat, load_sem.at[1])
@@ -133,14 +144,7 @@
         if c == OWN:
             w_loads[c].start()
 
-    barrier = pltpu.get_barrier_semaphore()
-    peers = [lax.rem(v + i, N_VOCAB) for i in range(1, N_VOCAB)]
-    row_peers = [lax.rem(r + i, N_ROWS) for i in range(1, N_ROWS)]
-    for p in peers:
-        pl.semaphore_signal(barrier, inc=1, device_id={"vocab": p}, device_id_type=MESH)
-    for p in row_peers:
-        pl.semaphore_signal(barrier, inc=1, device_id={"rows": p}, device_id_type=MESH)
-    pl.semaphore_wait(barrier, len(peers) + len(row_peers))
+    pl.semaphore_wait(barrier, 4 + len(row_peers))
 
     def send(link, c, r0, n):
         rows = pl.ds(r0, n)
@@ -172,7 +176,7 @@
             shared.add(group)
             wait_rows(sum(n for _, _, n in GROUPS[group]), share_recv.at[group])
 
-    def product(r0, size, chunks, first=False, seen=None):
+    def product(r0, size, chunks, first=False, seen=None, beside=()):
         for c in chunks:
             if c not in ready_w:
                 w_loads[c].wait()
@@ -182,6 +186,7 @@
                     if pc == c and p0 < r0 + size and r0 < p0 + n:
                         need(group)
         rows = slice(r0, r0 + size)
+        beside = list(beside)
         for j in range(0, WIDTH, TILE):
             cols = slice(j, min(j + TILE, WIDTH))
             t = None
@@ -192,8 +197,11 @@
             acc[rows, cols] = t
             if seen is not None:
                 seen(rows, cols.start, t)
-
-    def finish(q):
+            if beside:
+                beside.pop(0)()
+        assert not beside
+
+    def last_product(q, beside):
         mine_q = slice(q * Q, (q + 1) * Q)
         token = ids[mine_q, :]
         kept_bits = keeps[mine_q, :]
@@ -204,76 +212,66 @@
                 z = t[:, i * VBLK:(i + 1) * VBLK]
                 kz = jnp.where((kept_bits & (1 << b)) != 0, z, ABSENT)
                 hit = jnp.where(token == b * VBLK, z, 0.0)
-                kacc[:, b * VBLK:(b + 1) * VBLK] = kz
-                top[...] = z if b == 0 else jnp.maximum(top[...], z)
-                ktop[...] = kz if b == 0 else jnp.maximum(ktop[...], kz)
-                taken[...] = hit if b == 0 else taken[...] + hit
-
-        product(q * Q, Q, CROSS, seen=seen)
-        group = 32
-
-        def part(g, _):
-            rows = pl.ds(pl.multiple_of(q * Q + g * group, group), group)
-            here = pl.ds(pl.multiple_of(g * group, group), group)
-            m = top[here, :]
-            km = ktop[here, :]
+                kacc[mine_q, b * VBLK:(b + 1) * VBLK] = kz
+                top[mine_q, :] = z if b == 0 else jnp.maximum(top[mine_q, :], z)
+                ktop[mine_q, :] = kz if b == 0 else jnp.maximum(ktop[mine_q, :], kz)
+                taken[mine_q, :] = hit if b == 0 else taken[mine_q, :] + hit
+
+        product(q * Q, Q, CROSS, seen=seen, beside=beside)
+
+    def sums(q):
+        group = 16
+        steps = []
+
+        def part(r0):
+            rows = slice(r0, r0 + group)
+            m = top[rows, :]
+            km = ktop[rows, :]
             s = jnp.zeros((group, VBLK), F32)
             ks = jnp.zeros((group, VBLK), F32)
             for b in range(NBLK):
                 cols = slice(b * VBLK, (b + 1) * VBLK)
                 s += jnp.exp2((acc[rows, cols] - m) * EXP_SCALE)
-                ks += jnp.exp2((kacc[here, cols] - km) * EXP_SCALE)
-            total[here, :] = s
-            ktotal[here, :] = ks
-            return 0
-
-        lax.fori_loop(0, Q // group, part, 0)
-
-        def combined(maxes, sums):
-            mt = maxes[...].T
-            st = sums[...].T
+                ks += jnp.exp2((kacc[rows, cols] - km) * EXP_SCALE)
+            total[rows, :] = s
+            ktotal[rows, :] = ks
+
+        for r0 in range(q * Q, (q + 1) * Q, group):
+            steps.append(functools.partial(part, r0))
+        steps.append(functools.partial(combine, q))
+        return steps
+
+    def combine(q):
+        mine_q = slice(q * Q, (q + 1) * Q)
+
+        def combined(maxes, parts):
+            mt = maxes[mine_q, :].T
+            st = parts[mine_q, :].T
             best = jnp.max(mt, axis=0, keepdims=True)
             whole = jnp.sum(st * jnp.exp2((mt - best) * EXP_SCALE), axis=0, keepdims=True)
             return best / SOFTNESS + jnp.log(whole)
 
         full = combined(top, total)
         kept = combined(ktop, ktotal)
-        picked = jnp.sum(taken[...].T, axis=0, keepdims=True) / SOFTNESS
-        stats[q, v, 0:1, :] = full
-        stats[q, v, 1:2, :] = kept
-        stats[q, v, 2:3, :] = picked
-        stats[q, v, 3:4, :] = picked
-        for p in peers:
-            pltpu.make_async_remote_copy(
-                src_ref=stats.at[q, v], dst_ref=stats.at[q, v],
-                send_sem=stat_send, recv_sem=stat_recv.at[q],
-                device_id={"vocab": p}, device_id_type=MESH,
-            ).start()
-
-    def conclude(q):
-        others = stats.at[q, 0:N_VOCAB - 1]
-        pltpu.make_async_copy(others, others, stat_recv.at[q]).wait()
-        best = stats[q, 0]
-        for i in range(1, N_VOCAB):
-            best = jnp.maximum(best, stats[q, i])
-        whole = jnp.zeros((4, Q), F32)
-        chosen = jnp.zeros((4, Q), F32)
-        for i in range(N_VOCAB):
-            s = stats[q, i]
-            whole += jnp.exp(s - best)
-            chosen += s
-        lse = best + jnp.log(whole)
-        picked = chosen[2:3]
-        full = picked - lse[0:1]
-        kept = picked - lse[1:2]
-        out[q:q + 1, :] = full
-        out[NQ + q:NQ + q + 1, :] = kept
-        return kept - full
+        picked = jnp.sum(taken[mine_q, :].T, axis=0, keepdims=True) / SOFTNESS
+        stats[v, 0, q:q + 1, :] = full
+        stats[v, 1, q:q + 1, :] = kept
+        stats[v, 2, q:q + 1, :] = picked
+
+    def lse_of(i):
+        best = stats[0, i]
+        for d in range(1, N_VOCAB):
+            best = jnp.maximum(best, stats[d, i])
+        whole = jnp.exp(stats[0, i] - best)
+        for d in range(1, N_VOCAB):
+            whole += jnp.exp(stats[d, i] - best)
+        return best + jnp.log(whole)
 
     own_load.wait()
     ids_load.wait()
     bits_load.wait()
 
+    pending = []
     for step in PROGRAM:
         if step[0] == "send":
             send(*step[1:])
@@ -297,12 +295,26 @@
         elif step[0] == "mul":
             product(*step[1:])
         else:
-            finish(step[1])
-
-    gap = None
-    for q in range(NQ):
-        g = conclude(q)
-        gap = g if gap is None else gap + g
+            last_product(step[1], pending)
+            pending = sums(step[1])
+    for last_step in pending:
+        last_step()
+
+    for p in peers:
+        pltpu.make_async_remote_copy(
+            src_ref=stats.at[v], dst_ref=stats.at[v], send_sem=stat_send, recv_sem=stat_recv,
+            device_id={"vocab": p}, device_id_type=MESH,
+        ).start()
+    others = stats.at[0:N_VOCAB - 1]
+    pltpu.make_async_copy(others, others, stat_recv).wait()
+    picked = stats[0, 2]
+    for d in range(1, N_VOCAB):
+        picked += stats[d, 2]
+    full = picked - lse_of(0)
+    kept = picked - lse_of(1)
+    out[0:NQ, :] = full
+    out[NQ:2 * NQ, :] = kept
+    gap = jnp.sum(kept - full, axis=0, keepdims=True)
     gaps[r] = jnp.broadcast_to(gap, (8, Q))
     for p in row_peers:
         pltpu.make_async_remote_copy(
@@ -312,8 +324,7 @@
         ).start()
     everyone = h.at[:, pl.ds(0, ROWS * 15 // 16), :]
     pltpu.make_async_copy(everyone, everyone, send_sem).wait()
-    whole_stats = stats.at[:, 0:N_VOCAB - 1]
-    pltpu.make_async_copy(whole_stats, whole_stats, stat_send).wait()
+    pltpu.make_async_copy(others, others, stat_send).wait()
     others = gaps.at[0:N_ROWS - 1]
     pltpu.make_async_copy(others, others, gap_recv).wait()
     everything = gaps[0]
@@ -337,17 +348,17 @@
             pltpu.VMEM((CHIPS, ROWS, CHIP_FEAT), jnp.bfloat16),
             pltpu.VMEM((CHIPS, CHIP_FEAT, WIDTH), jnp.bfloat16),
             pltpu.VMEM((ROWS, WIDTH), F32),
-            pltpu.VMEM((Q, WIDTH), F32),
+            pltpu.VMEM((ROWS, WIDTH), F32),
             pltpu.VMEM((NQ, Q), jnp.int32),
             pltpu.VMEM((NQ, Q), jnp.int32),
             pltpu.VMEM((ROWS, VBLK), jnp.int32),
             pltpu.VMEM((ROWS, VBLK), jnp.int32),
-            pltpu.VMEM((Q, VBLK), F32),
-            pltpu.VMEM((Q, VBLK), F32),
-            pltpu.VMEM((Q, VBLK), F32),
-            pltpu.VMEM((Q, VBLK), F32),
-            pltpu.VMEM((Q, VBLK), F32),
-            pltpu.VMEM((NQ, N_VOCAB, 4, Q), F32),
+            pltpu.VMEM((ROWS, VBLK), F32),
+            pltpu.VMEM((ROWS, VBLK), F32),
+            pltpu.VMEM((ROWS, VBLK), F32),
+            pltpu.VMEM((ROWS, VBLK), F32),
+            pltpu.VMEM((ROWS, VBLK), F32),
+            pltpu.VMEM((N_VOCAB, 3, NQ, Q), F32),
             pltpu.VMEM((N_ROWS, 8, Q), F32),
             dma((3,)),
             dma((CHIPS,)),
@@ -355,7 +366,7 @@
             dma((len(GROUPS),)),
             dma((len(GROUPS) + 1,)),
             dma,
-            dma((NQ,)),
+            dma,
             dma,
             dma,
         ],

time: 44.9 us -> 43.3 us (0.964)
  Pallas kernels: 41.6 us -> 39.9 us
    pallas_call x1, Pallas kernels: 41.6 us -> 39.9 us  [per_device(): pl.pallas_call(kernel, out_shape=jax.ShapeDtypeStruct((2 * NQ + 1, Q), F3...]
where the time goes in v3:
time: 43.3 us; the launch traced here: 43.1 us
  Pallas kernels  39.9 us (92%)
  local copies, waits for them, and re-layouts  2.52 us (6%)
  between operations  0.64 us (1%)
    pallas_call x1, Pallas kernels, per_device(): pl.pallas_call(kernel, out_shape=jax.ShapeDtypeStruct((2 * NQ + 1, Q), F3...  39.9 us
    reshape x1, local copies, waits for them, and re-layouts, per_device(): out[NQ:2 * NQ].reshape(ROWS)  1.33 us
    slice x1, local copies, waits for them, and re-layouts, per_device(): out[2 * NQ, 0]  1.19 us

profile of v3, /device:TPU:1, one launch (start us, length us, event | category | flops | bytes accessed | tf_op | source)
XLA Modules:
  0.0 43.1 jit_solution(7128983865114481869)
XLA Ops:
  0.6 39.9 %shard_map.67 = f32[9,128]{1,0:T(8,128)} custom-call(bf16[512,256]{1,0:T(8,128)(2,1)} %hidden.1, bf16[4096,2432]{1,0:T(8,128)(2,1)} %weights.1, s32[4,128]{1,0:T(4,128)} %bitcast.7, s32[4,128]{1,0:T(4,128)} %bitcast.8), custom_call_target="tpu_custom_call" | custom-call | flops 10200547328 | bytes 19922944 | tf_op jit(solution)/shard_map/pallas_call | solution.py:342
  40.6 1.3 %slice_bitcast_fusion = (f32[512]{0:T(512)}, f32[512]{0:T(512)}) fusion(f32[9,128]{1,0:T(8,128)} %shard_map.67), kind=kLoop, calls=%fused_computation | loop fusion | bytes 8192 | tf_op jit(solution)/shard_map/reshape | solution.py:382
  41.9 1.2 %slice.11 = f32[1,1]{1,0:T(1,128)} slice(f32[9,128]{1,0:T(8,128)} %shard_map.67), slice={[8:9], [0:1]} | slice | bytes 8 | tf_op jit(solution)/shard_map/slice | solution.py:382

commit v4 on v3

--- a/solution.py
+++ b/solution.py
@@ -58,26 +58,28 @@
     ("send", "+", DOWN, 0, 128), ("send", "-", UP, 256, 128),
     ("send", "+", OWN, 384, 128), ("send", "-", OWN, 128, 128),
     ("got", ((XOWN, 0, 128),)),
+    ("mul", 0, 128, (DOWN,)),
+    ("mul", 256, 128, (UP,)),
     ("got", ((DOWN, 128, 128), (UP, 384, 128))),
     ("send", "+", DOWN, 128, 128), ("send", "-", UP, 384, 128),
     ("send", "+", XOWN, 0, 128), ("send", "-", XOWN, 0, 128),
-    ("mul", 0, 128, (DOWN, XOWN)),
     ("got", ((XOWN, 128, 128),)),
+    ("mul", 128, 128, (DOWN,)),
+    ("mul", 384, 128, (UP,)),
     ("got", ((DOWN, 256, 128), (UP, 0, 128))),
-    ("mul", 128, 128, (DOWN, XOWN)),
     ("got", ((FAR, 0, 128), (FAR, 256, 128))),
     ("send", "x", FAR, 0, 128), ("send", "x", FAR, 256, 128),
-    ("mul", 256, 256, (UP,)),
+    ("mul", 0, 128, (UP, XOWN)),
     ("got", ((XOWN, 256, 128), (XOWN, 384, 128))),
     ("send", "+", XOWN, 256, 128), ("send", "-", XOWN, 256, 128),
     ("send", "+", XOWN, 128, 128), ("send", "-", XOWN, 128, 128),
     ("send", "+", XOWN, 384, 128), ("send", "-", XOWN, 384, 128),
+    ("got", ((DOWN, 384, 128), (UP, 128, 128))),
     ("mul", 256, 128, (DOWN, XOWN)),
-    ("got", ((DOWN, 384, 128), (UP, 128, 128))),
     ("got", ((FAR, 128, 128), (FAR, 384, 128))),
     ("send", "x", FAR, 128, 128), ("send", "x", FAR, 384, 128),
+    ("mul", 128, 128, (UP, XOWN)),
     ("mul", 384, 128, (DOWN, XOWN)),
-    ("mul", 0, 256, (UP,)),
     ("mul", 0, 256, (FAR,)),
     ("got", at(CROSS, 0)),
     ("mul", 256, 256, (FAR,)),
@@ -330,8 +332,8 @@
     everything = gaps[0]
     for i in range(1, N_ROWS):
         everything += gaps[i]
-    mean = jnp.sum(everything[0:1], axis=1, keepdims=True) / TOKENS
-    out[2 * NQ:2 * NQ + 1, :] = jnp.broadcast_to(mean, (1, Q))
+    lane = lax.broadcasted_iota(jnp.int32, (NQ, Q), 0)
+    out[2 * NQ:, :] = jnp.where(lane == 0, everything[0:NQ] / TOKENS, 0.0)
     pltpu.make_async_copy(others, others, gap_send).wait()
 
 
@@ -341,7 +343,7 @@
     dma = pltpu.SemaphoreType.DMA
     out = pl.pallas_call(
         kernel,
-        out_shape=jax.ShapeDtypeStruct((2 * NQ + 1, Q), F32),
+        out_shape=jax.ShapeDtypeStruct((3 * NQ, Q), F32),
         in_specs=[anywhere] * 4,
         out_specs=vmem,
         scratch_shapes=[
@@ -379,7 +381,8 @@
             transcendentals=2 * ROWS * WIDTH,
         ),
     )(hidden, weights, sampled.reshape(NQ, Q), keep_bits.reshape(NQ, Q))
-    return out[:NQ].reshape(ROWS), out[NQ:2 * NQ].reshape(ROWS), out[2 * NQ, 0]
+    out = out.reshape(3, ROWS)
+    return out[0], out[1], jnp.sum(out[2])
 
 
 def solution(mesh):

time: 43.3 us -> 42.1 us (0.972)
  local copies, waits for them, and re-layouts: 2.52 us -> 0 us
  other arithmetic: 0 us -> 1.94 us
  Pallas kernels: 39.9 us -> 39.3 us
    reduce_sum x0 -> x1, other arithmetic: none -> 1.94 us  [per_device(): return (out[0], out[1], jnp.sum(out[2]))]
    reshape x1 -> x0, local copies, waits for them, and re-layouts: 1.33 us -> none  [per_device(): out[NQ:2 * NQ].reshape(ROWS)]
    slice x1 -> x0, local copies, waits for them, and re-layouts: 1.19 us -> none  [per_device(): out[2 * NQ, 0]]
    pallas_call x1, Pallas kernels: 39.9 us -> 39.3 us  [per_device(): pl.pallas_call(kernel, out_shape=jax.ShapeDtypeStruct((3 * NQ, Q), F32),...]
where the time goes in v4:
time: 42.1 us; the launch traced here: 41.9 us
  Pallas kernels  39.3 us (93%)
  other arithmetic  1.94 us (5%)
  between operations  0.64 us (2%)
    pallas_call x1, Pallas kernels, per_device(): pl.pallas_call(kernel, out_shape=jax.ShapeDtypeStruct((3 * NQ, Q), F32),...  39.3 us
    reduce_sum x1, other arithmetic, per_device(): return (out[0], out[1], jnp.sum(out[2]))  1.94 us

profile of v4, /device:TPU:1, one launch (start us, length us, event | category | flops | bytes accessed | tf_op | source)
XLA Modules:
  0.0 41.9 jit_solution(14084730384409602945)
XLA Ops:
  0.6 39.3 %shard_map.67 = f32[12,128]{1,0:T(8,128)} custom-call(bf16[512,256]{1,0:T(8,128)(2,1)} %hidden.1, bf16[4096,2432]{1,0:T(8,128)(2,1)} %weights.1, s32[4,128]{1,0:T(4,128)} %bitcast.6, s32[4,128]{1,0:T(4,128)} %bitcast.7), custom_call_target="tpu_custom_call" | custom-call | flops 10200547328 | bytes 19922944 | tf_op jit(solution)/shard_map/pallas_call | solution.py:344
  40.0 1.9 %slice_reduce_fusion = (f32[]{:T(128)}, f32[512]{0:T(512)}, f32[512]{0:T(512)}) fusion(f32[12,128]{1,0:T(8,128)} %shard_map.67), kind=kLoop, calls=%fused_computation | loop fusion | flops 511 | bytes 10244 | tf_op jit(solution)/shard_map/reduce_sum | solution.py:385

commit v5 on v4

--- a/solution.py
+++ b/solution.py
@@ -105,7 +105,7 @@
 def kernel(
     hidden, weights, sampled, bits,
     out,
-    h, w, acc, kacc, ids_flat, bits_flat, ids, keeps, top, ktop, total, ktotal, taken,
+    h, w, acc, ids_flat, bits_flat, ids, keeps, top, ktop, total, ktotal, taken,
     stats, gaps,
     load_sem, w_sem, send_sem, recv_sem, share_recv,
     stat_send, stat_recv, gap_send, gap_recv,
@@ -126,8 +126,19 @@
     target = {link: slot[d] * 2 + core for link, d in LINKS.items()}
 
     barrier = pltpu.get_barrier_semaphore()
-    peers = [lax.rem(v + i, N_VOCAB) for i in range(1, N_VOCAB)]
-    row_peers = [lax.rem(r + i, N_ROWS) for i in range(1, N_ROWS)]
+    hops = (0, 1, 2, 1)
+    places = [(dx, dy, dk) for dx in range(2) for dy in range(4) for dk in range(2)]
+    places.sort(key=lambda place: -2 * place[0] - hops[place[1]])
+    peers = [
+        slot[dx, dy] * 2 + lax.rem(core + dk, 2)
+        for dx, dy, dk in places
+        if (dx, dy, dk) != (0, 0, 0)
+    ]
+    row_places = [(dz, dx) for dz in range(4) for dx in range(2) if (dz, dx) != (0, 0)]
+    row_places.sort(key=lambda place: -hops[place[0]] - place[1])
+    row_peers = [
+        lax.rem(r // 2 + dz, 4) * 2 + lax.rem(lax.rem(r, 2) + dx, 2) for dz, dx in row_places
+    ]
     for p in (target["+"], target["-"], target["x"], sibling):
         pl.semaphore_signal(barrier, inc=1, device_id={"vocab": p}, device_id_type=MESH)
     for p in row_peers:
@@ -214,7 +225,6 @@
                 z = t[:, i * VBLK:(i + 1) * VBLK]
                 kz = jnp.where((kept_bits & (1 << b)) != 0, z, ABSENT)
                 hit = jnp.where(token == b * VBLK, z, 0.0)
-                kacc[mine_q, b * VBLK:(b + 1) * VBLK] = kz
                 top[mine_q, :] = z if b == 0 else jnp.maximum(top[mine_q, :], z)
                 ktop[mine_q, :] = kz if b == 0 else jnp.maximum(ktop[mine_q, :], kz)
                 taken[mine_q, :] = hit if b == 0 else taken[mine_q, :] + hit
@@ -234,7 +244,8 @@
             for b in range(NBLK):
                 cols = slice(b * VBLK, (b + 1) * VBLK)
                 s += jnp.exp2((acc[rows, cols] - m) * EXP_SCALE)
-                ks += jnp.exp2((kacc[rows, cols] - km) * EXP_SCALE)
+                kz = jnp.where((keeps[rows, :] & (1 << b)) != 0, acc[rows, cols], ABSENT)
+                ks += jnp.exp2((kz - km) * EXP_SCALE)
             total[rows, :] = s
             ktotal[rows, :] = ks
 
@@ -350,7 +361,6 @@
             pltpu.VMEM((CHIPS, ROWS, CHIP_FEAT), jnp.bfloat16),
             pltpu.VMEM((CHIPS, CHIP_FEAT, WIDTH), jnp.bfloat16),
             pltpu.VMEM((ROWS, WIDTH), F32),
-            pltpu.VMEM((ROWS, WIDTH), F32),
             pltpu.VMEM((NQ, Q), jnp.int32),
             pltpu.VMEM((NQ, Q), jnp.int32),
             pltpu.VMEM((ROWS, VBLK), jnp.int32),

time: 42.1 us -> 42 us (level)
  no operation moved by 1% of the time
where the time goes in v5:
time: 42 us; the launch traced here: 41.9 us
  Pallas kernels  39.3 us (94%)
  other arithmetic  1.94 us (5%)
  between operations  0.64 us (2%)
    pallas_call x1, Pallas kernels, per_device(): pl.pallas_call(kernel, out_shape=jax.ShapeDtypeStruct((3 * NQ, Q), F32),...  39.3 us
    reduce_sum x1, other arithmetic, per_device(): return (out[0], out[1], jnp.sum(out[2]))  1.94 us

profile of v5, /device:TPU:1, one launch (start us, length us, event | category | flops | bytes accessed | tf_op | source)
XLA Modules:
  0.0 41.9 jit_solution(13016297761236401888)
XLA Ops:
  0.6 39.3 %shard_map.67 = f32[12,128]{1,0:T(8,128)} custom-call(bf16[512,256]{1,0:T(8,128)(2,1)} %hidden.1, bf16[4096,2432]{1,0:T(8,128)(2,1)} %weights.1, s32[4,128]{1,0:T(4,128)} %bitcast.6, s32[4,128]{1,0:T(4,128)} %bitcast.7), custom_call_target="tpu_custom_call" | custom-call | flops 10200547328 | bytes 19922944 | tf_op jit(solution)/shard_map/pallas_call | solution.py:355
  39.9 1.9 %slice_reduce_fusion = (f32[]{:T(128)}, f32[512]{0:T(512)}, f32[512]{0:T(512)}) fusion(f32[12,128]{1,0:T(8,128)} %shard_map.67), kind=kLoop, calls=%fused_computation | loop fusion | flops 511 | bytes 10244 | tf_op jit(solution)/shard_map/reduce_sum | solution.py:395
